TPU v7x, 256 devices: a whole 4x4x8 slice. The times are simulated.
256 devices in a mesh: head: 8 (over y_hi, x), blk: 32 (over y_lo, z, core).
Axes of the slice: x: 4, y: 4 (y_hi: 2, y_lo: 2; y = y_hi * 2 + y_lo), z: 8, core: 2. Of those that a mesh axis runs over, the one named last changes fastest.
Arguments:
- queries: bfloat16 [32768, 3072], P(('blk', 'head')), may hold values from -120 to 120
- keys: bfloat16 [32768, 3072], P(('blk', 'head')), may hold values from -4 to 4
- values: bfloat16 [32768, 3072], P(('blk', 'head')), may hold values from -24 to 24
- text_codes: int32 [2, 256, 3072], P(None, None, 'head'), may hold values from -448 to 448
- text_exps: int32 [2, 256, 24], P(None, None, 'head'), may hold values from -9 to -7
Outputs:
- attended: bfloat16 [32768, 3072], P(('blk', 'head'))
All inputs are finite; a program needn't handle non-finite values.
Results may differ from a plain program's by a relative error of at most 0.0077.
Values may be sent and summed in bfloat16 or wider, within the bound.
A program may use at most 128 MiB of HBM per device.

v0:
```python
import math

import jax
import jax.numpy as jnp
from jax import lax
from jax.sharding import PartitionSpec as P

HD = 128
PREV = 3


def shifted(block, axis, distance):
    devices = range(lax.axis_size(axis))
    route = [((i - distance) % len(devices), i) for i in devices]
    return lax.ppermute(block, axis, route)


def dequantize(codes, exps):
    widened = jnp.repeat(exps.astype(jnp.float32), HD, axis=1)
    return (codes.astype(jnp.float32) * jnp.exp2(widened)).astype(jnp.bfloat16)


def attend(query_rows, window_keys, window_values):
    softmax_scale = 1.0 / math.sqrt(HD)
    row_count = query_rows.shape[0]
    group_heads = query_rows.shape[1] // HD
    block_size = min(512, row_count)
    query_tiles = query_rows.reshape(row_count // block_size, block_size, group_heads, HD)
    key_heads = window_keys.reshape(-1, group_heads, HD)
    value_heads = window_values.reshape(-1, group_heads, HD)

    def one_tile(query_tile):
        scores = (
            jnp.einsum("qhd,khd->hqk", query_tile, key_heads, preferred_element_type=jnp.float32)
            * softmax_scale
        )
        row_max = jnp.max(scores, axis=-1, keepdims=True)
        expo = jnp.exp(scores - row_max)
        total = jnp.sum(expo, axis=-1)
        weights = expo.astype(jnp.bfloat16)
        summed = jnp.einsum(
            "hqk,khd->qhd", weights, value_heads, preferred_element_type=jnp.float32
        )
        outcome = summed / jnp.transpose(total)[:, :, None]
        return outcome.astype(jnp.bfloat16).reshape(block_size, group_heads * HD)

    return lax.map(one_tile, query_tiles).reshape(row_count, group_heads * HD)


def local(queries, keys, values, text_codes, text_exps):
    stacked = jnp.stack((queries, keys, values))
    arrived = lax.all_to_all(stacked, "head", split_axis=2, concat_axis=1, tiled=True)
    query_rows = arrived[0]
    key_value = arrived[1:]
    text_keys = dequantize(text_codes[0], text_exps[0])
    text_values = dequantize(text_codes[1], text_exps[1])
    gathered = [key_value]
    carried = key_value
    for distance in range(PREV):
        carried = shifted(carried, "blk", 1)
        gathered.append(carried)
    window_keys = jnp.concatenate([member[0] for member in gathered] + [text_keys], axis=0)
    window_values = jnp.concatenate([member[1] for member in gathered] + [text_values], axis=0)
    outcome = attend(query_rows, window_keys, window_values)
    return lax.all_to_all(outcome, "head", split_axis=0, concat_axis=1, tiled=True)


def solution(mesh):
    in_specs = (
        P(("blk", "head"), None),
        P(("blk", "head"), None),
        P(("blk", "head"), None),
        P(None, None, "head"),
        P(None, None, "head"),
    )
    out_specs = P(("blk", "head"), None)
    return jax.shard_map(local, mesh=mesh, in_specs=in_specs, out_specs=out_specs, check_vma=False)
```

profile of v0, /device:TPU:8, one launch (start us, length us, event | category | flops | bytes accessed | tf_op | source)
XLA Modules:
  0.0 234.9 jit_solution(11487006766197290365)
XLA Ops:
  0.0 3.3 %pad_maximum_fusion = bf16[3,128,3072]{2,1,0:T(8,128)(2,1)} fusion(bf16[1,128,3072]{2,1,0:T(8,128)(2,1)} %bitcast.79, bf16[1,128,3072]{2,1,0:T(8,128)(2,1)} %bitcast.80, bf16[1,128,3072]{2,1,0:T(8,128)(2,1)} %bitcast.81), kind=kLoop, calls=%fused_computation.14 | loop fusion | flops 2359296 | bytes 4718592 | tf_op jit(solution)/shard_map/stack | solution.py:51
  3.3 4.4 %copy.33 = bf16[3,128,3072]{1,0,2:T(4,128)(2,1)S(1)} copy(bf16[3,128,3072]{2,1,0:T(8,128)(2,1)} %pad_maximum_fusion) | data formatting | bytes 4718592 | tf_op jit(solution)/shard_map/stack | solution.py:51
  7.6 45.5 %all_to_all.34 = bf16[3,128,3072]{1,0,2:T(4,128)(2,1)S(1)} all-to-all(bf16[3,128,3072]{1,0,2:T(4,128)(2,1)S(1)} %copy.33), channel_id=1, replica_groups=mesh['head'=8,'blk'=32] {'head'}, dimensions={2} | all-to-all | bytes 4718592 | tf_op jit(solution)/shard_map/all_to_all | solution.py:52
  53.2 1.9 copy.50
  55.1 1.2 slice.67
  56.4 0.0 copy-start.2
  56.4 3.7 %slice.53 = bf16[2,1024,384]{1,2,0:T(8,128)(2,1)} reshape(bf16[2,8,128,384]{2,1,3,0:T(8,128)(2,1)} %slice.67) | data formatting | bytes 3145728 | tf_op jit(solution)/shard_map/slice | solution.py:54
  60.1 0.0 collective-permute-start
  60.1 23.3 %collective-permute-done = bf16[2,1024,384]{1,2,0:T(8,128)(2,1)} collective-permute-done((bf16[2,1024,384]{1,2,0:T(8,128)(2,1)}, bf16[2,1024,384]{1,2,0:T(8,128)(2,1)}, u32[]{:S(2)}, u32[]{:S(2)}) %collective-permute-start) | collective-permute-done | bytes 1572896 | tf_op jit(solution)/shard_map/ppermute | solution.py:15
  83.4 0.0 collective-permute-start.1
  83.4 1.2 slice_convert_fusion
  84.6 1.0 copy.36
  85.5 0.2 copy.46
  85.7 0.0 copy-done.2
  85.8 19.9 %collective-permute-done.1 = bf16[2,1024,384]{1,2,0:T(8,128)(2,1)} collective-permute-done((bf16[2,1024,384]{1,2,0:T(8,128)(2,1)}, bf16[2,1024,384]{1,2,0:T(8,128)(2,1)}, u32[]{:S(2)}, u32[]{:S(2)}) %collective-permute-start.1) | collective-permute-done | bytes 1572896 | tf_op jit(solution)/shard_map/ppermute | solution.py:15
  105.7 0.0 collective-permute-start.2
  105.7 1.3 fusion.20
  107.0 1.4 concatenate.29
  108.4 1.4 concatenate.24
  109.8 0.3 reshape_squeeze.3
  110.1 1.8 copy.37
  111.9 0.1 constant_dynamic-update-slice_fusion.8
  112.0 1.0 constant_dynamic-update-slice_fusion.4
  112.9 1.5 fusion.23
  114.4 0.1 constant_dynamic-update-slice_fusion.7
  114.5 1.0 constant_dynamic-update-slice_fusion.3
  115.5 1.5 fusion.22
  117.0 0.1 constant_dynamic-update-slice_fusion.6
  117.0 0.0 copy-start
  117.0 1.1 constant_dynamic-update-slice_fusion.2
  118.2 9.8 %collective-permute-done.2 = bf16[2,1024,384]{1,2,0:T(8,128)(2,1)} collective-permute-done((bf16[2,1024,384]{1,2,0:T(8,128)(2,1)}, bf16[2,1024,384]{1,2,0:T(8,128)(2,1)}, u32[]{:S(2)}, u32[]{:S(2)}) %collective-permute-start.2) | collective-permute-done | bytes 1572896 | tf_op jit(solution)/shard_map/ppermute | solution.py:15
  127.9 2.4 %fusion.21 = (bf16[1,1024,384]{1,2,0:T(8,128)(2,1)}, bf16[1,1024,384]{1,2,0:T(8,128)(2,1)S(1)}) fusion(bf16[2,1024,384]{1,2,0:T(8,128)(2,1)} %collective-permute-done.2), kind=kLoop, calls=%fused_computation.34 | loop fusion | bytes 3145728 | tf_op jit(solution)/shard_map/slice | solution.py:63
  130.3 1.0 constant_dynamic-update-slice_fusion.1
  131.3 0.0 copy-done
  131.3 0.7 fusion.18
  132.0 4.6 %copy.38 = bf16[4352,3,128]{2,0,1:T(8,128)(2,1)S(1)} copy(bf16[4352,3,128]{0,2,1:T(8,128)(2,1)} %fusion.18) | data formatting | bytes 6684672 | tf_op jit(solution)/shard_map/while | solution.py:47
  136.6 2.2 constant_dynamic-update-slice_fusion.5
  138.8 1.7 fusion.19
  140.5 77.8 %while.10 = (s32[]{:T(128)}, bf16[2,512,384]{2,1,0:T(8,128)(2,1)}, bf16[2,512,3,128]{3,1,2,0:T(8,128)(2,1)}, bf16[4352,3,128]{2,0,1:T(8,128)(2,1)S(1)}, bf16[4352,3,128]{0,2,1:T(8,128)(2,1)}, /*index=5*/s32[]{:T(128)}) while((s32[]{:T(128)}, bf16[2,512,384]{2,1,0:T(8,128)(2,1)}, bf16[2,512,3,128]{3,1,2,0:T(8,128)(2,1)}, ...), condition=%wide.region_3.4_spmd, body=%wide.region_0.3_spmd.sunk | while | flops 3476419584 | bytes 102661216 | solution.py:47
  140.5 11.7 %multiply_reduce_fusion.2 = (f32[3,512]{1,0:T(4,128)S(1)}, f32[3,512,4352]{2,1,0:T(8,128)}) fusion(bf16[4352,3,128]{2,0,1:T(8,128)(2,1)S(1)} %get-tuple-element.130, bf16[2,512,3,128]{3,1,2,0:T(8,128)(2,1)} %get-tuple-element.129, s32[]{:T(128)} %get-tuple-element.121), kind=kOutput, calls=%fused_computation.1.clone.1 | convolution fusion | flops 1724643840 | bytes 30480896 | tf_op jit(solution)/shard_map/while/body/eval_jaxpr/qhd,khd->hqk/dot_general | solution.py:34
  152.2 0.0 copy-start.1
  152.2 11.4 %fusion.34 = f32[3,512]{1,0:T(4,128)S(1)} fusion(f32[3,512,4352]{2,1,0:T(8,128)} %get-tuple-element.113, f32[3,512]{1,0:T(4,128)S(1)} %get-tuple-element.114), kind=kLoop, calls=%fused_computation.2.clone.1 | loop fusion | flops 20052480 | bytes 26750976 | tf_op jit(solution)/shard_map/while/body/eval_jaxpr/reduce_sum | solution.py:39
  163.6 0.0 copy-done.1
  163.6 12.1 %fusion.35 = bf16[512,3,128]{0,2,1:T(8,128)(2,1)} fusion(bf16[4352,3,128]{0,2,1:T(8,128)(2,1)S(1)} %copy-done.1, f32[3,512,4352]{2,1,0:T(8,128)} %get-tuple-element.113, f32[3,512]{1,0:T(4,128)S(1)} %get-tuple-element.114, f32[512,3]{0,1:T(4,128)S(1)} %bitcast.83), kind=kOutput, calls=%fused_computation.7.clone.1 | convolution fusion | flops 1731723264 | bytes 30486528 | tf_op jit(solution)/shard_map/while/body/eval_jaxpr/hqk,khd->qhd/dot_general | solution.py:41
  175.7 1.9 copy.52
  177.6 1.8 constant_dynamic-update-slice_fusion.10
  179.4 11.7 %multiply_reduce_fusion.2 = (f32[3,512]{1,0:T(4,128)S(1)}, f32[3,512,4352]{2,1,0:T(8,128)}) fusion(bf16[4352,3,128]{2,0,1:T(8,128)(2,1)S(1)} %get-tuple-element.130, bf16[2,512,3,128]{3,1,2,0:T(8,128)(2,1)} %get-tuple-element.129, s32[]{:T(128)} %get-tuple-element.121), kind=kOutput, calls=%fused_computation.1.clone.1 | convolution fusion | flops 1724643840 | bytes 30480896 | tf_op jit(solution)/shard_map/while/body/eval_jaxpr/qhd,khd->hqk/dot_general | solution.py:34
  191.1 0.0 copy-start.1
  191.1 11.4 %fusion.34 = f32[3,512]{1,0:T(4,128)S(1)} fusion(f32[3,512,4352]{2,1,0:T(8,128)} %get-tuple-element.113, f32[3,512]{1,0:T(4,128)S(1)} %get-tuple-element.114), kind=kLoop, calls=%fused_computation.2.clone.1 | loop fusion | flops 20052480 | bytes 26750976 | tf_op jit(solution)/shard_map/while/body/eval_jaxpr/reduce_sum | solution.py:39
  202.5 0.0 copy-done.1
  202.5 12.1 %fusion.35 = bf16[512,3,128]{0,2,1:T(8,128)(2,1)} fusion(bf16[4352,3,128]{0,2,1:T(8,128)(2,1)S(1)} %copy-done.1, f32[3,512,4352]{2,1,0:T(8,128)} %get-tuple-element.113, f32[3,512]{1,0:T(4,128)S(1)} %get-tuple-element.114, f32[512,3]{0,1:T(4,128)S(1)} %bitcast.83), kind=kOutput, calls=%fused_computation.7.clone.1 | convolution fusion | flops 1731723264 | bytes 30486528 | tf_op jit(solution)/shard_map/while/body/eval_jaxpr/hqk,khd->qhd/dot_general | solution.py:41
  214.6 1.9 copy.52
  216.5 1.8 constant_dynamic-update-slice_fusion.10
  218.3 15.1 %all_to_all.35 = bf16[8,128,384]{2,1,0:T(8,128)(2,1)S(1)} all-to-all(bf16[8,128,384]{2,1,0:T(8,128)(2,1)} %bitcast.82), channel_id=1, replica_groups=mesh['head'=8,'blk'=32] {'head'}, dimensions={0} | all-to-all | bytes 1572864 | tf_op jit(solution)/shard_map/all_to_all | solution.py:65
  233.3 0.4 copy.40
  233.7 1.2 copy.41
  (4 shorter events, 0.1 us)
Async XLA Ops:
  56.4 29.4 %copy-start.2 = (s32[2,256,3]{1,0,2:T(2,128)S(1)}, s32[2,256,3]{1,0,2:T(2,128)}, u32[]{:S(2)}) copy-start(s32[2,256,3]{1,0,2:T(2,128)} %param.11) | copy-start | bytes 18436
  60.1 23.3 %collective-permute-start = (bf16[2,1024,384]{1,2,0:T(8,128)(2,1)}, bf16[2,1024,384]{1,2,0:T(8,128)(2,1)}, u32[]{:S(2)}, u32[]{:S(2)}) collective-permute-start(bf16[2,1024,384]{1,2,0:T(8,128)(2,1)} %slice.53), channel_id=1, source_target_pairs={{31,0},{0,1},{1,2},{2,3},{3,4},{4,5},{5,6},{6,7},{7,8},{8,9},{9,10... | collective-permute-start | bytes 4718600 | tf_op jit(solution)/shard_map/ppermute | solution.py:15
  83.4 22.3 %collective-permute-start.1 = (bf16[2,1024,384]{1,2,0:T(8,128)(2,1)}, bf16[2,1024,384]{1,2,0:T(8,128)(2,1)}, u32[]{:S(2)}, u32[]{:S(2)}) collective-permute-start(bf16[2,1024,384]{1,2,0:T(8,128)(2,1)} %collective-permute-done), channel_id=1, source_target_pairs={{31,0},{0,1},{1,2},{2,3},{3,4},{4,5},{5,6},{6,7},{7,8},{8,9},{9,10... | collective-permute-start | bytes 4718600 | tf_op jit(solution)/shard_map/ppermute | solution.py:15
  105.7 22.3 %collective-permute-start.2 = (bf16[2,1024,384]{1,2,0:T(8,128)(2,1)}, bf16[2,1024,384]{1,2,0:T(8,128)(2,1)}, u32[]{:S(2)}, u32[]{:S(2)}) collective-permute-start(bf16[2,1024,384]{1,2,0:T(8,128)(2,1)} %collective-permute-done.1), channel_id=1, source_target_pairs={{31,0},{0,1},{1,2},{2,3},{3,4},{4,5},{5,6},{6,7},{7,8},{8,9},{9,10... | collective-permute-start | bytes 4718600 | tf_op jit(solution)/shard_map/ppermute | solution.py:15
  117.0 14.3 %copy-start = (bf16[4352,3,128]{0,2,1:T(8,128)(2,1)}, bf16[4352,3,128]{0,2,1:T(8,128)(2,1)S(1)}, u32[]{:S(2)}) copy-start(bf16[4352,3,128]{0,2,1:T(8,128)(2,1)S(1)} %constant_dynamic-update-slice_fusion.6) | copy-start | bytes 10027012
  152.2 11.4 %copy-start.1 = (bf16[4352,3,128]{0,2,1:T(8,128)(2,1)S(1)}, bf16[4352,3,128]{0,2,1:T(8,128)(2,1)}, u32[]{:S(2)}) copy-start(bf16[4352,3,128]{0,2,1:T(8,128)(2,1)} %get-tuple-element.131) | copy-start | bytes 10027012 | tf_op jit(solution)/shard_map/while
  191.1 11.4 %copy-start.1 = (bf16[4352,3,128]{0,2,1:T(8,128)(2,1)S(1)}, bf16[4352,3,128]{0,2,1:T(8,128)(2,1)}, u32[]{:S(2)}) copy-start(bf16[4352,3,128]{0,2,1:T(8,128)(2,1)} %get-tuple-element.131) | copy-start | bytes 10027012 | tf_op jit(solution)/shard_map/while
where the time goes:
time: 236 us; the launch traced here: 235 us
  blocking collectives  60.6 us (26%)
  waiting for transfers between devices  53 us (22%)
  matrix products  47.5 us (20%)
  local copies, waits for them, and re-layouts  43.8 us (19%)
  other arithmetic  29.8 us (13%)
    ppermute x3, waiting for transfers between devices, shifted(): return lax.ppermute(block, axis, route)  53 us
    all_to_all x1, blocking collectives, local(): lax.all_to_all(stacked, 'head', split_axis=2, concat_axis=1, tiled=True)  45.5 us
    dot_general x2, matrix products, one_tile(): jnp.einsum('hqk,khd->qhd', weights, value_heads, preferred_element_type=j...  24.2 us
    dot_general x2, matrix products, one_tile(): jnp.einsum('qhd,khd->hqk', query_tile, key_heads, preferred_element_type=...  23.4 us
    reduce_sum x2, other arithmetic, one_tile(): total = jnp.sum(expo, axis=-1)  22.8 us
    all_to_all x1, blocking collectives, local(): lax.all_to_all(outcome, 'head', split_axis=0, concat_axis=1, tiled=True)  15.1 us
    dynamic_update_slice x4, local copies, waits for them, and re-layouts, attend(): return lax.map(one_tile, query_tiles).reshape(row_count, group_heads * HD)  7.36 us
    slice x4, local copies, waits for them, and re-layouts, local(): member[1]  6.65 us
  transfers between devices with their start and end apart: 3, of which 3 were waited for; matrix products, arithmetic and copies ran while one was open for 6% of the time, Pallas kernels for 0%

commit v1 on v0

v1 whole, which is shorter than its diff:
```python
import math

import jax
import jax.numpy as jnp
from jax import lax
from jax.experimental import pallas as pl
from jax.experimental.pallas import tpu as pltpu
from jax.sharding import PartitionSpec as P

HD = 128
ROWS = 128
BLOCK = 1024
TEXT = 256
GROUP = 8
N_BLK = 32
PAIRS = 16
A_SLOTS, B_SLOTS = 5, 4
TILE = 256
CHUNK = 512
MESH = pl.DeviceIdType.MESH
SCALE = math.log2(math.e) / math.sqrt(HD)
BF16, F32 = jnp.bfloat16, jnp.float32


def owner(t, p):
    return (t * 8 + p % 8) * 2 + p // 8


def kernel(
    q_in, k_in, v_in, codes_in, exps_in, out,
    qs, ks, vs, tks, tvs, codes, exps, m_s, acc_s, o_s,
    text_sem, k_sem, v_sem, q_sem, out_sem,
    piece_send, own_send, fwd_send, o_send, o_own_send,
):
    me = lax.axis_index("head")
    b = lax.axis_index("blk")
    yl, z, c = b // 16, (b // 2) % 8, b % 2
    pair, pair_q = b // 2, ((b + N_BLK - 1) % N_BLK) // 2
    mine = c * 8 + z
    after, after2 = (b + 1) % N_BLK, (b + 2) % N_BLK
    before, before2 = (b + N_BLK - 1) % N_BLK, (b + N_BLK - 2) % N_BLK
    next_a, prev_a = owner(yl, (mine + 1) % PAIRS), owner(yl, (mine + PAIRS - 1) % PAIRS)

    text_copies = [
        pltpu.make_async_copy(codes_in.at[:, :, pl.ds(pl.multiple_of(yl * HD, HD), HD)], codes.at[0], text_sem.at[0]),
        pltpu.make_async_copy(codes_in.at[:, :, pl.ds(2 * HD, HD)], codes.at[1], text_sem.at[1]),
        pltpu.make_async_copy(exps_in, exps, text_sem.at[2]),
    ]
    for copy in text_copies:
        copy.start()

    barrier = pltpu.get_barrier_semaphore()

    def tell(head, blk):
        pl.semaphore_signal(barrier, inc=1, device_id=(head, blk), device_id_type=MESH)

    def greet(i, _):
        other = (me + 1 + i) % GROUP
        for d in range(3):
            tell(other, (mine * 2 + d) % N_BLK)
        tell(other, b)
        tell(other, after)
        tell(other, before)
        for t in range(2):
            tell(other, owner(t, pair_q))
        return 0

    lax.fori_loop(0, GROUP - 1, greet, 0)
    for d in range(3):

        @pl.when((mine * 2 + d) % N_BLK != b)
        def _():
            tell(me, (mine * 2 + d) % N_BLK)

    for t in range(2):

        @pl.when(owner(t, pair_q) != b)
        def _():
            tell(me, owner(t, pair_q))

    tell(me, after)
    tell(me, before)
    tell(me, before2)
    tell(me, next_a)
    tell(me, prev_a)
    expected = 16 * (2 - c) + 7 + 8 + 16 + 8 + 3
    expected = expected - jnp.where(yl == c, 1, 0) - jnp.where((yl == 1) & (c == 1), 1, 0)
    pl.semaphore_wait(barrier, expected)

    def column(head):
        return pl.ds(pl.multiple_of(head * HD, HD), HD)

    def piece(source, head, target, row, sems, slot, to, send_sem):
        return pltpu.make_async_remote_copy(
            src_ref=source.at[:, column(head)],
            dst_ref=target.at[pl.ds(pl.multiple_of(row, ROWS), ROWS)],
            send_sem=send_sem,
            recv_sem=sems.at[slot],
            device_id=to,
            device_id_type=MESH,
        )

    def stay(source, head, target, row, sems, slot):
        return pltpu.make_async_copy(
            source.at[:, column(head)], target.at[pl.ds(pl.multiple_of(row, ROWS), ROWS)], sems.at[slot]
        )

    key_slot, query_slot = 2 + c, (b + 1) % 2

    def scatter_a(tensor, source, target, sems, slot, to_pair):
        row = slot * BLOCK + me * ROWS

        def send(i, _):
            j = (me + 1 + i) % GROUP
            for t in range(2):
                piece(source, 3 * j + t, target, row, sems, slot, (j, owner(t, to_pair)), piece_send.at[tensor]).start()
            return 0

        lax.fori_loop(0, GROUP - 1, send, 0)
        for t in range(2):

            @pl.when(owner(t, to_pair) != b)
            def _():
                piece(source, 3 * me + t, target, row, sems, slot, (me, owner(t, to_pair)), own_send.at[tensor, t]).start()

            @pl.when(owner(t, to_pair) == b)
            def _():
                stay(source, 3 * me + t, target, row, sems, slot).start()

    def scatter_b(tensor, source, target, sems, slot, to_blk, count):
        row = slot * BLOCK + me * ROWS

        def send(i, _):
            j = (me + 1 + i) % GROUP
            piece(source, 3 * j + 2, target, row, sems, slot, (j, to_blk), piece_send.at[tensor]).start()
            return 0

        lax.fori_loop(0, count, send, 0)

    scatter_a(0, k_in, ks, k_sem, key_slot, pair)
    scatter_a(2, q_in, qs, q_sem, query_slot, pair_q)
    scatter_a(1, v_in, vs, v_sem, key_slot, pair)
    scatter_b(0, k_in, ks, k_sem, A_SLOTS + 2, b, GROUP - 1)
    stay(k_in, 3 * me + 2, ks, (A_SLOTS + 2) * BLOCK + me * ROWS, k_sem, A_SLOTS + 2).start()
    scatter_b(1, v_in, vs, v_sem, A_SLOTS + 2, b, GROUP - 1)
    stay(v_in, 3 * me + 2, vs, (A_SLOTS + 2) * BLOCK + me * ROWS, v_sem, A_SLOTS + 2).start()
    scatter_b(2, q_in, qs, q_sem, 2, before, GROUP)

    for copy in text_copies:
        copy.wait()
    for u in range(2):
        for i, target in enumerate((tks, tvs)):
            if u:
                exponent = exps[i, :, 2:3]
            else:
                exponent = jnp.where(yl == 0, exps[i, :, 0:1], exps[i, :, 1:2])
            target[u] = (codes[u, i].astype(F32) * jnp.exp2(exponent.astype(F32))).astype(BF16)
    m_s[...] = jnp.full(m_s.shape, -1e30, F32)
    acc_s[...] = jnp.zeros(acc_s.shape, F32)

    def block(ref, slot, rows=BLOCK):
        return ref.at[pl.ds(pl.multiple_of(slot * BLOCK, BLOCK), rows)]

    def arrived(ref, sems, slot):
        pltpu.make_async_copy(block(ref, slot), block(ref, slot), sems.at[slot]).wait()

    def forward(ref, sems, slot, to_slot, to_blk, send):
        return pltpu.make_async_remote_copy(
            src_ref=block(ref, slot),
            dst_ref=block(ref, to_slot),
            send_sem=fwd_send.at[send],
            recv_sem=sems.at[to_slot],
            device_id=(me, to_blk),
            device_id_type=MESH,
        )

    ONE, ZERO, THREE, TWO = A_SLOTS + 1, A_SLOTS, A_SLOTS + 3, A_SLOTS + 2
    forwards_a, forwards_even, forwards_odd, relays = [], [], [], []
    for i, (ref, sems) in enumerate(((ks, k_sem), (vs, v_sem))):
        forwards_a.append((
            forward(ref, sems, 2, 0, next_a, 7 * i),
            forward(ref, sems, 3, 1, next_a, 7 * i + 1),
            forward(ref, sems, 2, 4, prev_a, 7 * i + 2),
        ))
        forwards_even.append((
            forward(ref, sems, TWO, ZERO, after2, 7 * i + 3),
            forward(ref, sems, TWO, THREE, before, 7 * i + 4),
            forward(ref, sems, TWO, ONE, after, 7 * i + 5),
        ))
        forwards_odd.append((
            forward(ref, sems, TWO, ZERO, after2, 7 * i + 3),
            forward(ref, sems, TWO, THREE, before, 7 * i + 4),
        ))
        relays.append(forward(ref, sems, ZERO, ONE, before, 7 * i + 6))

    def pass_on_a(i, ref, sems):
        arrived(ref, sems, 2)
        forwards_a[i][0].start()
        forwards_a[i][2].start()
        arrived(ref, sems, 3)
        forwards_a[i][1].start()

    def pass_on_b(i, ref, sems):
        arrived(ref, sems, TWO)

        @pl.when(c == 0)
        def _():
            for copy in forwards_even[i]:
                copy.start()

        @pl.when(c == 1)
        def _():
            for copy in forwards_odd[i]:
                copy.start()

    def attend(query, keys, values, chunks):
        for i in range(BLOCK // TILE):
            rows = pl.ds(pl.multiple_of(query * BLOCK + i * TILE, TILE), TILE)
            q, m, acc = qs[rows, :], m_s[rows, :], acc_s[rows, :]
            for at, size in chunks:
                span = pl.ds(pl.multiple_of(at, size), size)
                k, v = keys[span, :], values[span, :]
                s = lax.dot_general(q, k, (((1,), (1,)), ((), ())), preferred_element_type=F32)
                m_new = jnp.maximum(m, jnp.max(s, axis=1, keepdims=True))
                p = jnp.exp2((s - jnp.concatenate([m_new] * (size // HD), axis=1)) * SCALE).astype(BF16)
                alpha = jnp.exp2((m - m_new) * SCALE)
                wide = jnp.concatenate([v, jnp.ones((size, HD), BF16)], axis=1)
                acc = acc * jnp.concatenate([alpha, alpha], axis=1) + jnp.dot(p, wide, preferred_element_type=F32)
                m = m_new
            m_s[rows, :] = m
            acc_s[rows, :] = acc

    def image(query, slot):
        attend(query, ks, vs, [(slot * BLOCK + n * CHUNK, CHUNK) for n in range(BLOCK // CHUNK)])

    def text(query, unit):
        attend(query, tks.at[unit], tvs.at[unit], [(0, TEXT)])

    def result(query, r, head, to_blk, send_sem):
        rows = pl.ds(pl.multiple_of(query * BLOCK + r * ROWS, ROWS), ROWS)
        return pltpu.make_async_remote_copy(
            src_ref=o_s.at[rows],
            dst_ref=out.at[:, column(head)],
            send_sem=send_sem,
            recv_sem=out_sem.at[0],
            device_id=(r, to_blk),
            device_id_type=MESH,
        )

    def finish(query, head, to_blk, count):
        rows = pl.ds(query * BLOCK, BLOCK)
        o_s[rows, :] = (acc_s[rows, :HD] / acc_s[rows, HD:]).astype(BF16)

        def send(i, _):
            result(query, (me + 1 + i) % GROUP, head, to_blk, o_send.at[query]).start()
            return 0

        lax.fori_loop(0, count, send, 0)

    def finish_a(query):
        head, to_blk = 3 * me + yl, (mine * 2 + 1 + query) % N_BLK
        finish(query, head, to_blk, GROUP - 1)

        @pl.when(to_blk != b)
        def _():
            result(query, me, head, to_blk, o_own_send.at[query]).start()

        @pl.when(to_blk == b)
        def _():
            rows = pl.ds(pl.multiple_of(query * BLOCK + me * ROWS, ROWS), ROWS)
            pltpu.make_async_copy(o_s.at[rows], out.at[:, column(head)], out_sem.at[0]).start()

    def own_blocks(query):
        def step(slot, _):
            image(query, slot)
            return 0

        lax.fori_loop(2, 4, step, 0)

    pass_on_a(0, ks, k_sem)
    arrived(qs, q_sem, 0)
    pass_on_a(1, vs, v_sem)
    own_blocks(0)
    text(0, 0)
    pass_on_b(0, ks, k_sem)
    arrived(qs, q_sem, 1)
    own_blocks(1)
    text(1, 0)
    pass_on_b(1, vs, v_sem)
    arrived(qs, q_sem, 2)
    text(2, 1)

    image(2, TWO)
    arrived(ks, k_sem, 4)
    arrived(vs, v_sem, 4)
    image(1, 4)
    arrived(ks, k_sem, THREE)
    arrived(vs, v_sem, THREE)
    image(2, THREE)
    arrived(ks, k_sem, 1)
    arrived(vs, v_sem, 1)

    def step_one(query, _):
        image(query, 1)
        return 0

    lax.fori_loop(0, 2, step_one, 0)
    finish_a(1)
    arrived(ks, k_sem, 0)
    arrived(vs, v_sem, 0)
    image(0, 0)
    finish_a(0)

    @pl.when(c == 1)
    def _():
        arrived(ks, k_sem, ZERO)
        relays[0].start()
        arrived(vs, v_sem, ZERO)
        relays[1].start()

    arrived(ks, k_sem, ONE)
    arrived(vs, v_sem, ONE)

    @pl.when(c == 0)
    def _():
        arrived(ks, k_sem, ZERO)
        arrived(vs, v_sem, ZERO)

    def step_last(slot, _):
        image(2, slot)
        return 0

    lax.fori_loop(ZERO, ONE + 1, step_last, 0)
    finish(2, 3 * me + 2, after, GROUP)

    def sent(sem, ref):
        pltpu.make_async_copy(ref, ref, sem).wait()

    sent(piece_send.at[0], ks.at[pl.ds(0, 21 * ROWS)])
    sent(piece_send.at[1], ks.at[pl.ds(0, 21 * ROWS)])
    sent(piece_send.at[2], ks.at[pl.ds(0, 22 * ROWS)])
    for tensor, to_pair in ((0, pair), (1, pair), (2, pair_q)):
        for t in range(2):

            @pl.when(owner(t, to_pair) != b)
            def _():
                sent(own_send.at[tensor, t], ks.at[pl.ds(0, ROWS)])

    for i in range(2):
        for copy in forwards_a[i]:
            copy.wait_send()

        @pl.when(c == 0)
        def _():
            for copy in forwards_even[i]:
                copy.wait_send()

        @pl.when(c == 1)
        def _():
            for copy in forwards_odd[i]:
                copy.wait_send()
            relays[i].wait_send()

    for query in range(2):
        sent(o_send.at[query], o_s.at[pl.ds(0, (GROUP - 1) * ROWS)])

        @pl.when((mine * 2 + 1 + query) % N_BLK != b)
        def _():
            sent(o_own_send.at[query], o_s.at[pl.ds(0, ROWS)])

    sent(o_send.at[2], o_s.at[pl.ds(0, GROUP * ROWS)])
    pltpu.make_async_copy(out, out, out_sem.at[0]).wait()


def local(queries, keys, values, text_codes, text_exps):
    slots = A_SLOTS + B_SLOTS
    dma = pltpu.SemaphoreType.DMA
    return pl.pallas_call(
        kernel,
        out_shape=jax.ShapeDtypeStruct(queries.shape, BF16),
        in_specs=[pl.BlockSpec(memory_space=pl.ANY)] * 5,
        out_specs=pl.BlockSpec(memory_space=pl.ANY),
        scratch_shapes=[
            pltpu.VMEM((3 * BLOCK, HD), BF16),
            pltpu.VMEM((slots * BLOCK, HD), BF16),
            pltpu.VMEM((slots * BLOCK, HD), BF16),
            pltpu.VMEM((2, TEXT, HD), BF16),
            pltpu.VMEM((2, TEXT, HD), BF16),
            pltpu.VMEM((2, 2, TEXT, HD), jnp.int32),
            pltpu.VMEM(text_exps.shape, jnp.int32),
            pltpu.VMEM((3 * BLOCK, HD), F32),
            pltpu.VMEM((3 * BLOCK, 2 * HD), F32),
            pltpu.VMEM((3 * BLOCK, HD), BF16),
            dma((3,)),
            dma((slots,)),
            dma((slots,)),
            dma((3,)),
            dma((1,)),
            dma((3,)),
            dma((3, 2)),
            dma((14,)),
            dma((3,)),
            dma((2,)),
        ],
        compiler_params=pltpu.CompilerParams(collective_id=0, has_side_effects=True, vmem_limit_bytes=50 << 20),
        cost_estimate=pl.CostEstimate(flops=7 * 10**9, bytes_accessed=4 * 10**6, transcendentals=14 * 10**6),
    )(queries, keys, values, text_codes, text_exps)


def solution(mesh):
    rows = P(("blk", "head"), None)
    text = P(None, None, "head")
    return jax.shard_map(
        local, mesh=mesh, in_specs=(rows, rows, rows, text, text), out_specs=rows, check_vma=False
    )
```

time: 236 us -> 84.4 us (0.36)
  the two profiles are of different devices: /device:TPU:8 before, /device:TPU:1 now
where the time goes in v1:
time: 84.4 us; the launch traced here: 84 us
  Pallas kernels  78.9 us (93%)
  local copies, waits for them, and re-layouts  5.11 us (6%)
    pallas_call x1, Pallas kernels, local(): pl.pallas_call(kernel, out_shape=jax.ShapeDtypeStruct(queries.shape, BF16...  78.9 us
    unnamed x8, local copies, waits for them, and re-layouts  5.11 us

profile of v1, /device:TPU:1, one launch (start us, length us, event | category | flops | bytes accessed | tf_op | source)
XLA Modules:
  0.0 84.0 jit_solution(12747007604710185584)
XLA Ops:
  0.0 0.8 copy.6.exps_in
  0.8 0.0 copy-start
  0.8 1.1 %copy-done = bf16[128,3072]{1,0:T(8,128)(2,1)S(1)} copy-done((bf16[128,3072]{1,0:T(8,128)(2,1)S(1)}, bf16[128,3072]{1,0:T(8,128)(2,1)}, u32[]{:S(2)}) %copy-start) | copy-done | bytes 786456
  2.0 0.0 copy-start.1
  2.0 1.1 %copy-done.1 = bf16[128,3072]{1,0:T(8,128)(2,1)S(1)} copy-done((bf16[128,3072]{1,0:T(8,128)(2,1)S(1)}, bf16[128,3072]{1,0:T(8,128)(2,1)}, u32[]{:S(2)}) %copy-start.1) | copy-done | bytes 786456
  3.1 0.0 copy-start.2
  3.1 1.1 %copy-done.2 = bf16[128,3072]{1,0:T(8,128)(2,1)S(1)} copy-done((bf16[128,3072]{1,0:T(8,128)(2,1)S(1)}, bf16[128,3072]{1,0:T(8,128)(2,1)}, u32[]{:S(2)}) %copy-start.2) | copy-done | bytes 786456
  4.2 78.9 %shard_map.55 = bf16[128,3072]{1,0:T(8,128)(2,1)S(1)} custom-call(bf16[128,3072]{1,0:T(8,128)(2,1)S(1)} %copy-done, bf16[128,3072]{1,0:T(8,128)(2,1)S(1)} %copy-done.1, bf16[128,3072]{1,0:T(8,128)(2,1)S(1)} %copy-done.2, s32[2,256,384]{2,1,0:T(8,128)} %codes_in.1, s32[2,256,3]{2,1,0:T(8,128)S(1)} %copy.6.exps_in), custom_call_target="tpu_custom_call" | custom-call | flops 7000000000 | bytes 4000000 | tf_op jit(solution)/shard_map/pallas_call | solution.py:378
  83.1 0.9 %copy.8 = bf16[128,3072]{1,0:T(8,128)(2,1)} copy(bf16[128,3072]{1,0:T(8,128)(2,1)S(1)} %shard_map.55) | data formatting | bytes 1572864
Async XLA Ops:
  0.8 1.1 %copy-start = (bf16[128,3072]{1,0:T(8,128)(2,1)S(1)}, bf16[128,3072]{1,0:T(8,128)(2,1)}, u32[]{:S(2)}) copy-start(bf16[128,3072]{1,0:T(8,128)(2,1)} %q_in.1) | copy-start | bytes 2359300
  2.0 1.1 %copy-start.1 = (bf16[128,3072]{1,0:T(8,128)(2,1)S(1)}, bf16[128,3072]{1,0:T(8,128)(2,1)}, u32[]{:S(2)}) copy-start(bf16[128,3072]{1,0:T(8,128)(2,1)} %k_in.1) | copy-start | bytes 2359300
  3.1 1.1 %copy-start.2 = (bf16[128,3072]{1,0:T(8,128)(2,1)S(1)}, bf16[128,3072]{1,0:T(8,128)(2,1)}, u32[]{:S(2)}) copy-start(bf16[128,3072]{1,0:T(8,128)(2,1)} %v_in.1) | copy-start | bytes 2359300

commit v2 on v1

--- a/solution.py
+++ b/solution.py
@@ -138,23 +138,17 @@
         lax.fori_loop(0, count, send, 0)
 
     scatter_a(0, k_in, ks, k_sem, key_slot, pair)
-    scatter_a(2, q_in, qs, q_sem, query_slot, pair_q)
     scatter_a(1, v_in, vs, v_sem, key_slot, pair)
-    scatter_b(0, k_in, ks, k_sem, A_SLOTS + 2, b, GROUP - 1)
-    stay(k_in, 3 * me + 2, ks, (A_SLOTS + 2) * BLOCK + me * ROWS, k_sem, A_SLOTS + 2).start()
-    scatter_b(1, v_in, vs, v_sem, A_SLOTS + 2, b, GROUP - 1)
-    stay(v_in, 3 * me + 2, vs, (A_SLOTS + 2) * BLOCK + me * ROWS, v_sem, A_SLOTS + 2).start()
-    scatter_b(2, q_in, qs, q_sem, 2, before, GROUP)
-
     for copy in text_copies:
         copy.wait()
     for u in range(2):
         for i, target in enumerate((tks, tvs)):
             if u:
-                exponent = exps[i, :, 2:3]
+                exponent = exps[2, i : i + 1, :]
             else:
-                exponent = jnp.where(yl == 0, exps[i, :, 0:1], exps[i, :, 1:2])
-            target[u] = (codes[u, i].astype(F32) * jnp.exp2(exponent.astype(F32))).astype(BF16)
+                exponent = jnp.where(yl == 0, exps[0, i : i + 1, :], exps[1, i : i + 1, :])
+            scales = jnp.broadcast_to(jnp.exp2(exponent.astype(F32)), (HD, TEXT)).T
+            target[u] = (codes[u, i].astype(F32) * scales).astype(BF16)
     m_s[...] = jnp.full(m_s.shape, -1e30, F32)
     acc_s[...] = jnp.zeros(acc_s.shape, F32)
 
@@ -278,8 +272,14 @@
         lax.fori_loop(2, 4, step, 0)
 
     pass_on_a(0, ks, k_sem)
+    scatter_a(2, q_in, qs, q_sem, query_slot, pair_q)
+    pass_on_a(1, vs, v_sem)
+    scatter_b(0, k_in, ks, k_sem, A_SLOTS + 2, b, GROUP - 1)
+    stay(k_in, 3 * me + 2, ks, (A_SLOTS + 2) * BLOCK + me * ROWS, k_sem, A_SLOTS + 2).start()
+    scatter_b(1, v_in, vs, v_sem, A_SLOTS + 2, b, GROUP - 1)
+    stay(v_in, 3 * me + 2, vs, (A_SLOTS + 2) * BLOCK + me * ROWS, v_sem, A_SLOTS + 2).start()
+    scatter_b(2, q_in, qs, q_sem, 2, before, GROUP)
     arrived(qs, q_sem, 0)
-    pass_on_a(1, vs, v_sem)
     own_blocks(0)
     text(0, 0)
     pass_on_b(0, ks, k_sem)
@@ -387,7 +387,7 @@
             pltpu.VMEM((2, TEXT, HD), BF16),
             pltpu.VMEM((2, TEXT, HD), BF16),
             pltpu.VMEM((2, 2, TEXT, HD), jnp.int32),
-            pltpu.VMEM(text_exps.shape, jnp.int32),
+            pltpu.VMEM((3, 2, TEXT), jnp.int32),
             pltpu.VMEM((3 * BLOCK, HD), F32),
             pltpu.VMEM((3 * BLOCK, 2 * HD), F32),
             pltpu.VMEM((3 * BLOCK, HD), BF16),
@@ -402,9 +402,9 @@
             dma((3,)),
             dma((2,)),
         ],
-        compiler_params=pltpu.CompilerParams(collective_id=0, has_side_effects=True, vmem_limit_bytes=50 << 20),
+        compiler_params=pltpu.CompilerParams(collective_id=0, has_side_effects=True, vmem_limit_bytes=63 << 20),
         cost_estimate=pl.CostEstimate(flops=7 * 10**9, bytes_accessed=4 * 10**6, transcendentals=14 * 10**6),
-    )(queries, keys, values, text_codes, text_exps)
+    )(queries, keys, values, text_codes, jnp.transpose(text_exps, (2, 0, 1)))
 
 
 def solution(mesh):

time: 84.4 us -> 72.6 us (0.86)
  Pallas kernels: 78.9 us -> 70.4 us
  local copies, waits for them, and re-layouts: 5.11 us -> 2.06 us
    pallas_call x1, Pallas kernels: 78.9 us -> 70.4 us  [local(): pl.pallas_call(kernel, out_shape=jax.ShapeDtypeStruct(queries.shape, BF16...]
    unnamed x8 -> x1, local copies, waits for them, and re-layouts: 5.11 us -> 2.06 us
where the time goes in v2:
time: 72.6 us; the launch traced here: 72.5 us
  Pallas kernels  70.4 us (97%)
  local copies, waits for them, and re-layouts  2.06 us (3%)
    pallas_call x1, Pallas kernels, local(): pl.pallas_call(kernel, out_shape=jax.ShapeDtypeStruct(queries.shape, BF16...  70.4 us
    unnamed x1, local copies, waits for them, and re-layouts  2.06 us

profile of v2, /device:TPU:1, one launch (start us, length us, event | category | flops | bytes accessed | tf_op | source)
XLA Modules:
  0.0 72.5 jit_solution(7556816219495797606)
XLA Ops:
  0.0 70.4 %shard_map.55 = bf16[128,3072]{1,0:T(8,128)(2,1)} custom-call(bf16[128,3072]{1,0:T(8,128)(2,1)} %q_in.1, bf16[128,3072]{1,0:T(8,128)(2,1)} %k_in.1, bf16[128,3072]{1,0:T(8,128)(2,1)} %v_in.1, s32[2,256,384]{2,1,0:T(8,128)} %codes_in.1, s32[3,2,256]{2,1,0:T(2,128)} %bitcast.1), custom_call_target="tpu_custom_call" | custom-call | flops 7000000000 | bytes 4000000 | tf_op jit(solution)/shard_map/pallas_call | solution.py:378
  70.4 2.1 %copy.7 = bf16[128,3072]{1,0:T(8,128)(2,1)} copy(bf16[128,3072]{1,0:T(8,128)(2,1)} %shard_map.55) | data formatting | bytes 1572864

commit v3 on v2

--- a/solution.py
+++ b/solution.py
@@ -196,6 +196,8 @@
 
     def pass_on_b(i, ref, sems):
         arrived(ref, sems, TWO)
+        forwards_a[i][0].wait_send()
+        forwards_a[i][1].wait_send()
 
         @pl.when(c == 0)
         def _():
@@ -347,8 +349,7 @@
                 sent(own_send.at[tensor, t], ks.at[pl.ds(0, ROWS)])
 
     for i in range(2):
-        for copy in forwards_a[i]:
-            copy.wait_send()
+        forwards_a[i][2].wait_send()
 
         @pl.when(c == 0)
         def _():

time: 72.6 us -> 70.8 us (0.975)
  Pallas kernels: 70.4 us -> 68.7 us
    pallas_call x1, Pallas kernels: 70.4 us -> 68.7 us  [local(): pl.pallas_call(kernel, out_shape=jax.ShapeDtypeStruct(queries.shape, BF16...]
where the time goes in v3:
time: 70.8 us; the launch traced here: 70.7 us
  Pallas kernels  68.7 us (97%)
  local copies, waits for them, and re-layouts  2.06 us (3%)
    pallas_call x1, Pallas kernels, local(): pl.pallas_call(kernel, out_shape=jax.ShapeDtypeStruct(queries.shape, BF16...  68.7 us
    unnamed x1, local copies, waits for them, and re-layouts  2.06 us

profile of v3, /device:TPU:1, one launch (start us, length us, event | category | flops | bytes accessed | tf_op | source)
XLA Modules:
  0.0 70.7 jit_solution(9617378790795311143)
XLA Ops:
  0.0 68.7 %shard_map.55 = bf16[128,3072]{1,0:T(8,128)(2,1)} custom-call(bf16[128,3072]{1,0:T(8,128)(2,1)} %q_in.1, bf16[128,3072]{1,0:T(8,128)(2,1)} %k_in.1, bf16[128,3072]{1,0:T(8,128)(2,1)} %v_in.1, s32[2,256,384]{2,1,0:T(8,128)} %codes_in.1, s32[3,2,256]{2,1,0:T(2,128)} %bitcast.1), custom_call_target="tpu_custom_call" | custom-call | flops 7000000000 | bytes 4000000 | tf_op jit(solution)/shard_map/pallas_call | solution.py:379
  68.7 2.1 %copy.7 = bf16[128,3072]{1,0:T(8,128)(2,1)} copy(bf16[128,3072]{1,0:T(8,128)(2,1)} %shard_map.55) | data formatting | bytes 1572864

commit v4 on v3

--- a/solution.py
+++ b/solution.py
@@ -299,6 +299,13 @@
     arrived(ks, k_sem, THREE)
     arrived(vs, v_sem, THREE)
     image(2, THREE)
+
+    @pl.when(c == 1)
+    def _():
+        arrived(ks, k_sem, ONE)
+        arrived(vs, v_sem, ONE)
+        image(2, ONE)
+
     arrived(ks, k_sem, 1)
     arrived(vs, v_sem, 1)
 
@@ -313,26 +320,26 @@
     image(0, 0)
     finish_a(0)
 
+    arrived(ks, k_sem, ZERO)
+
     @pl.when(c == 1)
     def _():
-        arrived(ks, k_sem, ZERO)
         relays[0].start()
-        arrived(vs, v_sem, ZERO)
+
+    arrived(vs, v_sem, ZERO)
+
+    @pl.when(c == 1)
+    def _():
         relays[1].start()
 
-    arrived(ks, k_sem, ONE)
-    arrived(vs, v_sem, ONE)
+    image(2, ZERO)
 
     @pl.when(c == 0)
     def _():
-        arrived(ks, k_sem, ZERO)
-        arrived(vs, v_sem, ZERO)
-
-    def step_last(slot, _):
-        image(2, slot)
-        return 0
-
-    lax.fori_loop(ZERO, ONE + 1, step_last, 0)
+        arrived(ks, k_sem, ONE)
+        arrived(vs, v_sem, ONE)
+        image(2, ONE)
+
     finish(2, 3 * me + 2, after, GROUP)
 
     def sent(sem, ref):

time: 70.8 us -> 70.8 us (level)
  no operation moved by 1% of the time
where the time goes in v4:
time: 70.8 us; the launch traced here: 70.7 us
  Pallas kernels  68.6 us (97%)
  local copies, waits for them, and re-layouts  2.06 us (3%)
    pallas_call x1, Pallas kernels, local(): pl.pallas_call(kernel, out_shape=jax.ShapeDtypeStruct(queries.shape, BF16...  68.6 us
    unnamed x1, local copies, waits for them, and re-layouts  2.06 us

profile of v4, /device:TPU:1, one launch (start us, length us, event | category | flops | bytes accessed | tf_op | source)
XLA Modules:
  0.0 70.7 jit_solution(14472234100250634289)
XLA Ops:
  0.0 68.6 %shard_map.55 = bf16[128,3072]{1,0:T(8,128)(2,1)} custom-call(bf16[128,3072]{1,0:T(8,128)(2,1)} %q_in.1, bf16[128,3072]{1,0:T(8,128)(2,1)} %k_in.1, bf16[128,3072]{1,0:T(8,128)(2,1)} %v_in.1, s32[2,256,384]{2,1,0:T(8,128)} %codes_in.1, s32[3,2,256]{2,1,0:T(2,128)} %bitcast.1), custom_call_target="tpu_custom_call" | custom-call | flops 7000000000 | bytes 4000000 | tf_op jit(solution)/shard_map/pallas_call | solution.py:386
  68.6 2.1 %copy.7 = bf16[128,3072]{1,0:T(8,128)(2,1)} copy(bf16[128,3072]{1,0:T(8,128)(2,1)} %shard_map.55) | data formatting | bytes 1572864

commit v5 on v4

--- a/solution.py
+++ b/solution.py
@@ -196,18 +196,22 @@
 
     def pass_on_b(i, ref, sems):
         arrived(ref, sems, TWO)
-        forwards_a[i][0].wait_send()
-        forwards_a[i][1].wait_send()
 
         @pl.when(c == 0)
         def _():
-            for copy in forwards_even[i]:
+            for copy in forwards_even[i][1:]:
                 copy.start()
 
         @pl.when(c == 1)
         def _():
-            for copy in forwards_odd[i]:
+            for copy in forwards_odd[i][1:]:
                 copy.start()
+
+        if i:
+            for n in range(2):
+                forwards_a[n][0].wait_send()
+                forwards_a[n][1].wait_send()
+                forwards_even[n][0].start()
 
     def attend(query, keys, values, chunks):
         for i in range(BLOCK // TILE):
@@ -357,15 +361,16 @@
 
     for i in range(2):
         forwards_a[i][2].wait_send()
+        forwards_even[i][0].wait_send()
 
         @pl.when(c == 0)
         def _():
-            for copy in forwards_even[i]:
+            for copy in forwards_even[i][1:]:
                 copy.wait_send()
 
         @pl.when(c == 1)
         def _():
-            for copy in forwards_odd[i]:
+            for copy in forwards_odd[i][1:]:
                 copy.wait_send()
             relays[i].wait_send()
 

time: 70.8 us -> 70.9 us (level)
  no operation moved by 1% of the time
where the time goes in v5:
time: 70.9 us; the launch traced here: 70.8 us
  Pallas kernels  68.7 us (97%)
  local copies, waits for them, and re-layouts  2.06 us (3%)
    pallas_call x1, Pallas kernels, local(): pl.pallas_call(kernel, out_shape=jax.ShapeDtypeStruct(queries.shape, BF16...  68.7 us
    unnamed x1, local copies, waits for them, and re-layouts  2.06 us

profile of v5, /device:TPU:1, one launch (start us, length us, event | category | flops | bytes accessed | tf_op | source)
XLA Modules:
  0.0 70.8 jit_solution(4093193604872191262)
XLA Ops:
  0.0 68.7 %shard_map.55 = bf16[128,3072]{1,0:T(8,128)(2,1)} custom-call(bf16[128,3072]{1,0:T(8,128)(2,1)} %q_in.1, bf16[128,3072]{1,0:T(8,128)(2,1)} %k_in.1, bf16[128,3072]{1,0:T(8,128)(2,1)} %v_in.1, s32[2,256,384]{2,1,0:T(8,128)} %codes_in.1, s32[3,2,256]{2,1,0:T(2,128)} %bitcast.1), custom_call_target="tpu_custom_call" | custom-call | flops 7000000000 | bytes 4000000 | tf_op jit(solution)/shard_map/pallas_call | solution.py:391
  68.7 2.1 %copy.7 = bf16[128,3072]{1,0:T(8,128)(2,1)} copy(bf16[128,3072]{1,0:T(8,128)(2,1)} %shard_map.55) | data formatting | bytes 1572864
